TPU v7x, 32 devices: a whole 2x2x4 slice. The times are simulated.
32 devices in a mesh: req: 2 (over x), tile: 16 (over z, y, core).
Axes of the slice: x: 2, y: 2, z: 4, core: 2. Of those that a mesh axis runs over, the one named last changes fastest.
Arguments:
- queries: bfloat16 [32, 512, 384], P(('req', 'tile')), parts along dimension 0, may hold values from -12 to 12
- keys: bfloat16 [32, 512, 384], P(('req', 'tile')), parts along dimension 0, may hold values from -5 to 5
- values: bfloat16 [32, 512, 384], P(('req', 'tile')), parts along dimension 0, may hold values from -6 to 6
- text_keys: bfloat16 [512, 1536], P(('req', 'tile')), parts along dimension 0, may hold values from -6 to 6
- text_values: bfloat16 [512, 1536], P(('req', 'tile')), parts along dimension 0, may hold values from -6 to 6
- text_mask: int32 [512], P(('req', 'tile')), parts along dimension 0, may hold values 0 or 1
Outputs:
- attended: bfloat16 [32, 512, 384], P(('req', 'tile')), parts along dimension 0
There are 2 independent parts, one for each index of `req`. A program takes and returns all parts, laid end to end along the dimension named above; each array names one. Nothing has to cross between parts.
All inputs are finite; a program needn't handle non-finite values. No bound on the sum of `text_mask` on one device may be relied on, other than what follows from the above.
Results may differ from a plain program's by a relative error of at most 0.004.
Values may be sent and summed in bfloat16 or wider, within the bound.
A program may use at most 192 MiB of HBM per device.

v0:
```python
import functools
import math

import jax
import jax.numpy as jnp
from jax import lax
from jax.experimental import pallas as pl
from jax.experimental.pallas import tpu as pltpu
from jax.sharding import PartitionSpec as P

MESH = pl.DeviceIdType.MESH
EXP2_SCALE = math.log2(math.e) / math.sqrt(128)

TS = 8
HEAD_DIM = 128
HEAD_GROUPS = 4


MASKED = -1e30


def passed_along(value, axis, steps):
    count = lax.axis_size(axis)
    first, last = (max(0, -steps), min(count, count - steps))
    return lax.ppermute(value, axis, [(source, source + steps) for source in range(first, last)])


def shortened(value):
    return jax.tree.map(lambda a: a.astype(jnp.bfloat16) if a.dtype == jnp.float32 else a, value)


def fold_block(running, query_heads, key_block, value_block, key_keep):
    row_top, row_total, summed = running
    head_count = query_heads.shape[1]
    key_heads = key_block.reshape(key_block.shape[0], head_count, HEAD_DIM)
    value_heads = value_block.reshape(value_block.shape[0], head_count, HEAD_DIM)
    scores = jnp.einsum("qhd,khd->hqk", query_heads, key_heads, preferred_element_type=jnp.float32)
    scores = scores * (1.0 / math.sqrt(HEAD_DIM))
    scores = jnp.where(key_keep[None, None, :], scores, MASKED)
    new_top = jnp.maximum(row_top, jnp.max(scores, axis=-1))
    scale_down = jnp.exp(row_top - new_top)
    exp_terms = jnp.where(key_keep[None, None, :], jnp.exp(scores - new_top[:, :, None]), 0.0)
    row_total = row_total * scale_down + jnp.sum(exp_terms, axis=-1)
    weights = exp_terms.astype(jnp.bfloat16)
    summed = summed * scale_down[:, :, None] + jnp.einsum(
        "hqk,khd->hqd", weights, value_heads, preferred_element_type=jnp.float32
    )
    return (new_top, row_total, summed)


def gathered_shards(queries, keys, values, text_keys, text_values, text_mask):
    tokens = queries.shape[1]
    lane_width = queries.shape[2]
    head_count = lane_width // HEAD_DIM
    query_heads = queries[0].reshape(tokens, head_count, HEAD_DIM)
    own_pair = jnp.stack([keys[0], values[0]])
    group_count = HEAD_GROUPS
    tiles_all = lax.axis_size("tile") // group_count
    grid_w = min(4, tiles_all)
    grid_h = min(4, tiles_all // grid_w)
    grid_f = tiles_all // (grid_w * grid_h)
    frames_valid = grid_f * TS - TS // 4
    my_index = lax.axis_index("tile")
    tile_id = my_index // group_count
    head_group = my_index % group_count
    w_pos = tile_id % grid_w
    h_pos = tile_id // grid_w % grid_h
    f_pos = tile_id // (grid_w * grid_h)
    local_frame = jnp.arange(tokens, dtype=jnp.int32) // (TS * TS)

    def keep_mask(off_frame, off_height, off_width):
        inside = (
            (f_pos + off_frame >= 0)
            & (f_pos + off_frame < grid_f)
            & (h_pos + off_height >= 0)
            & (h_pos + off_height < grid_h)
            & (w_pos + off_width >= 0)
            & (w_pos + off_width < grid_w)
        )
        return inside & ((f_pos + off_frame) * TS + local_frame < frames_valid)

    running = (
        jnp.full((head_count, tokens), MASKED, jnp.float32),
        jnp.zeros((head_count, tokens), jnp.float32),
        jnp.zeros((head_count, tokens, HEAD_DIM), jnp.float32),
    )
    text_flags = text_mask.astype(jnp.bfloat16)
    piece_keys = lax.dynamic_slice_in_dim(
        lax.all_gather(text_keys, "tile", axis=0, tiled=True),
        head_group * lane_width,
        lane_width,
        1,
    )
    piece_values = lax.dynamic_slice_in_dim(
        lax.all_gather(text_values, "tile", axis=0, tiled=True),
        head_group * lane_width,
        lane_width,
        1,
    )
    running = fold_block(
        running,
        query_heads,
        piece_keys,
        piece_values,
        lax.all_gather(text_flags, "tile", axis=0, tiled=True) > 0.5,
    )
    running = fold_block(running, query_heads, own_pair[0], own_pair[1], keep_mask(0, 0, 0))
    width_set = {0: own_pair}
    for off_width in (-1, 1):
        width_set[off_width] = passed_along(own_pair, "tile", -off_width * group_count)
    width_offsets = sorted(width_set)
    row_stack = jnp.stack([width_set[spot] for spot in width_offsets])
    height_set = {0: row_stack}
    if grid_h > 1:
        for off_height in (-1, 1):
            height_set[off_height] = passed_along(
                shortened(row_stack), "tile", -off_height * grid_w * group_count
            ).astype(row_stack.dtype)
    height_offsets = sorted(height_set)
    slab_stack = jnp.stack([height_set[spot] for spot in height_offsets])

    def fold_slab(state_now, slab_pairs, off_frame):
        for h_slot, off_height in enumerate(height_offsets):
            for w_slot, off_width in enumerate(width_offsets):
                if off_frame == 0 and off_height == 0 and (off_width == 0):
                    continue
                state_now = fold_block(
                    state_now,
                    query_heads,
                    slab_pairs[h_slot, w_slot, 0],
                    slab_pairs[h_slot, w_slot, 1],
                    keep_mask(off_frame, off_height, off_width),
                )
        return state_now

    running = fold_slab(running, slab_stack, 0)
    if grid_f > 1:
        for off_frame in (-1, 1):
            got_slab = passed_along(
                shortened(slab_stack), "tile", -off_frame * grid_h * grid_w * group_count
            ).astype(slab_stack.dtype)
            running = fold_slab(running, got_slab, off_frame)
    row_top, row_total, summed = running
    result = summed / row_total[:, :, None]
    result = jnp.transpose(result, (1, 0, 2)).reshape(tokens, lane_width)
    return result.astype(jnp.bfloat16)[None]


def row_kernel(
    count, rows_kept, head_count, text_rows,
    q_hbm, k_hbm, v_hbm, tk_hbm, tv_hbm, mask_hbm, out_hbm,
    q_ref, k_ref, v_ref, tk_ref, tv_ref, mask_ref, packets, flags_in, text, near_k, near_v, out_ref,
    top_ref, total_ref, summed_ref,
    in_sem, out_sem, plane_send, plane_recv, chain_send, chain_recv, near_send, near_recv,
):
    groups = HEAD_GROUPS
    tiles = count // groups
    per_source = 2 * head_count
    flag_at = groups * per_source
    me = lax.axis_index("tile")
    tile = me // groups
    group = lax.rem(me, groups)
    first_here = tile * groups
    has_left = tile > 0
    has_right = tile < tiles - 1
    target = (me + groups, me - groups)
    sends = (has_right, has_left)
    receives = (has_left, has_right)

    def partner(step):
        return first_here + lax.rem(group + step, groups)

    barrier = pltpu.get_barrier_semaphore()
    for step in range(1, groups):
        pl.semaphore_signal(barrier, inc=1, device_id={"tile": partner(step)}, device_id_type=MESH)
    for side in range(2):

        @pl.when(sends[side])
        def _():
            pl.semaphore_signal(barrier, inc=1, device_id={"tile": target[side]}, device_id_type=MESH)

    loads = [
        pltpu.make_async_copy(mask_hbm, mask_ref, in_sem.at[0]),
        pltpu.make_async_copy(tk_hbm, tk_ref, in_sem.at[1]),
        pltpu.make_async_copy(tv_hbm, tv_ref, in_sem.at[2]),
        pltpu.make_async_copy(q_hbm.at[0], q_ref, in_sem.at[3]),
        pltpu.make_async_copy(k_hbm.at[0, pl.ds(0, rows_kept), :], k_ref, in_sem.at[4]),
        pltpu.make_async_copy(v_hbm.at[0, pl.ds(0, rows_kept), :], v_ref, in_sem.at[5]),
    ]
    for load in loads:
        load.start()

    def near_copy(side, head, which):
        cols = pl.ds(head * HEAD_DIM, HEAD_DIM)
        source, landing = ((k_hbm, near_k), (v_hbm, near_v))[which]
        return pltpu.make_async_remote_copy(
            src_ref=source.at[0, pl.ds(0, rows_kept), cols],
            dst_ref=landing.at[side, :, cols],
            send_sem=near_send.at[side, head, which],
            recv_sem=near_recv.at[side, head, which],
            device_id={"tile": target[side]},
            device_id_type=MESH,
        )

    def start_near(head, which):
        for side in range(2):

            @pl.when(sends[side])
            def _():
                near_copy(side, head, which).start()

    def plane_copies(step):
        to = partner(step)
        made = []
        for which, (source, landing) in enumerate(
            (
                (packets.at[lax.rem(group + step, groups)], text.at[tile, pl.ds(group * per_source, per_source)]),
                (flags_in.at[group], flags_in.at[group]),
            )
        ):
            made.append(
                pltpu.make_async_remote_copy(
                    src_ref=source,
                    dst_ref=landing,
                    send_sem=plane_send.at[step, which],
                    recv_sem=plane_recv.at[step, which],
                    device_id={"tile": to},
                    device_id_type=MESH,
                )
            )
        return made

    def chain_copy(side, hop, owner):
        return pltpu.make_async_remote_copy(
            src_ref=text.at[owner],
            dst_ref=text.at[owner],
            send_sem=chain_send.at[side, hop],
            recv_sem=chain_recv.at[side, hop],
            device_id={"tile": target[side]},
            device_id_type=MESH,
        )

    def chain_sent(side, hop):
        owner = tile - hop if side == 0 else tile + hop
        there = owner >= 0 if side == 0 else owner < tiles
        return owner, there & sends[side]

    def chain_got(side, hop):
        owner = tile - hop - 1 if side == 0 else tile + hop + 1
        return owner, owner >= 0 if side == 0 else owner < tiles

    def start_chain(hop):
        for side in range(2):
            owner, there = chain_sent(side, hop)

            @pl.when(there)
            def _():
                chain_copy(side, hop, owner).start()

    def wait_chain(hop):
        for side in range(2):
            owner, there = chain_got(side, hop)

            @pl.when(there)
            def _():
                chain_copy(side, hop, owner).wait_recv()

    def fold(head, keys, values, keep, first):
        query = q_ref[:, head * HEAD_DIM : (head + 1) * HEAD_DIM]
        scores = lax.dot_general(query, keys, (((1,), (1,)), ((), ())), preferred_element_type=jnp.float32)
        if keep is not None:
            scores = jnp.where(keep, scores, MASKED)
        block_top = jnp.broadcast_to(jnp.max(scores, axis=1, keepdims=True), (scores.shape[0], HEAD_DIM))
        new_top = block_top if first else jnp.maximum(top_ref[head], block_top)
        pieces = [
            jnp.exp2((scores[:, at : at + HEAD_DIM] - new_top) * EXP2_SCALE) for at in range(0, keys.shape[0], HEAD_DIM)
        ]
        part = functools.reduce(lambda a, b: a + b, pieces)
        weights = jnp.concatenate([piece.astype(jnp.bfloat16) for piece in pieces], axis=1)
        product = jnp.dot(weights, values, preferred_element_type=jnp.float32)
        if first:
            total_ref[head] = part
            summed_ref[head] = product
        else:
            scale_down = jnp.exp2((top_ref[head] - new_top) * EXP2_SCALE)
            total_ref[head] = total_ref[head] * scale_down + part
            summed_ref[head] = summed_ref[head] * scale_down + product
        top_ref[head] = new_top

    def fold_near(head):
        cols = slice(head * HEAD_DIM, (head + 1) * HEAD_DIM)
        for side in range(2):

            @pl.when(receives[side])
            def _():
                for which in range(2):
                    near_copy(side, head, which).wait_recv()
                fold(head, near_k[side, :, cols], near_v[side, :, cols], None, False)

    def out_copy(head):
        cols = pl.ds(head * HEAD_DIM, HEAD_DIM)
        return pltpu.make_async_copy(out_ref.at[:, cols], out_hbm.at[0, :, cols], out_sem.at[head])

    loads[0].wait()
    row_of = lax.broadcasted_iota(jnp.int32, (text_rows, HEAD_DIM), 0)
    lane_of = lax.broadcasted_iota(jnp.int32, (text_rows, HEAD_DIM), 1)
    flags = jnp.zeros((text_rows, HEAD_DIM), jnp.float32)
    for row in range(text_rows):
        flags = jnp.where((row_of == row) & (lane_of == me), mask_ref[row].astype(jnp.float32), flags)
    flags_in[group] = flags.astype(jnp.bfloat16)
    loads[1].wait()
    loads[2].wait()
    for to in range(groups):
        for which, source in enumerate((tk_ref, tv_ref)):
            for head in range(head_count):
                at = (to * head_count + head) * HEAD_DIM
                packets[to, which * head_count + head] = source[:, at : at + HEAD_DIM]
    text[tile, pl.ds(group * per_source, per_source)] = packets[group]

    pl.semaphore_wait(barrier, groups - 1 + has_left.astype(jnp.int32) + has_right.astype(jnp.int32))

    for step in range(1, groups):
        for copy in plane_copies(step):
            copy.start()
    start_near(0, 0)
    start_near(0, 1)
    for step in range(1, groups):
        for copy in plane_copies(step):
            copy.wait_recv()
    text[tile, flag_at] = functools.reduce(lambda a, b: a + b, [flags_in[source] for source in range(groups)])
    start_chain(0)
    start_near(1, 0)

    for load in loads[3:]:
        load.wait()
    for head in range(head_count):
        cols = slice(head * HEAD_DIM, (head + 1) * HEAD_DIM)
        fold(head, k_ref[:, cols], v_ref[:, cols], None, True)

    rest = [(1, 1)] + [(head, which) for head in range(2, head_count) for which in range(2)]
    folded = 0
    for hop in range(1, tiles - 1):
        wait_chain(hop - 1)
        start_chain(hop)
        if rest:
            start_near(*rest.pop(0))
        if hop == tiles - 2:
            for item in rest:
                start_near(*item)
        if folded < head_count - 1:
            fold_near(folded)
            folded += 1
    wait_chain(tiles - 2)

    wide_row = lax.broadcasted_iota(jnp.int32, (count * text_rows, HEAD_DIM), 0)
    wide_lane = lax.broadcasted_iota(jnp.int32, (count * text_rows, HEAD_DIM), 1)
    spread = jnp.concatenate([text[source // groups, flag_at] for source in range(count)], axis=0)
    spread = jnp.where(wide_lane == wide_row // text_rows, spread, jnp.zeros_like(spread))
    keep_row = lax.dot_general(
        jnp.ones((8, HEAD_DIM), jnp.bfloat16), spread, (((1,), (1,)), ((), ())), preferred_element_type=jnp.float32
    )[0:1, :]
    keep = jnp.broadcast_to(keep_row, (q_ref.shape[0], keep_row.shape[1])) > 0.5

    def text_piece(at):
        return jnp.concatenate(
            [text[source // groups, source % groups * per_source + at] for source in range(count)], axis=0
        )

    for head in range(head_count):
        fold(head, text_piece(head), text_piece(head_count + head), keep, False)

    for head in range(head_count):
        if head >= folded:
            fold_near(head)
        cols = slice(head * HEAD_DIM, (head + 1) * HEAD_DIM)
        total = jnp.sum(total_ref[head], axis=1, keepdims=True)
        out_ref[:, cols] = (summed_ref[head] / total).astype(out_ref.dtype)
        out_copy(head).start()

    for step in range(1, groups):
        for copy in plane_copies(step):
            copy.wait_send()
    for side in range(2):

        @pl.when(sends[side])
        def _():
            for head in range(head_count):
                for which in range(2):
                    near_copy(side, head, which).wait_send()

        for hop in range(tiles - 1):
            owner, there = chain_sent(side, hop)

            @pl.when(there)
            def _():
                chain_copy(side, hop, owner).wait_send()

    for head in range(head_count):
        out_copy(head).wait()


def row_shards(queries, keys, values, text_keys, text_values, text_mask):
    tokens, width = queries.shape[1:]
    head_count = width // HEAD_DIM
    count = lax.axis_size("tile")
    tiles = count // HEAD_GROUPS
    text_rows = text_keys.shape[0]
    rows_kept = (TS - TS // 4) * TS * TS
    bf16, f32 = jnp.bfloat16, jnp.float32
    dma = pltpu.SemaphoreType.DMA
    hbm = pl.BlockSpec(memory_space=pltpu.HBM)
    keys_seen = 3 * rows_kept + count * text_rows
    per_source = 2 * head_count
    return pl.pallas_call(
        functools.partial(row_kernel, count, rows_kept, head_count, text_rows),
        out_shape=jax.ShapeDtypeStruct(queries.shape, bf16),
        in_specs=[hbm] * 6,
        out_specs=hbm,
        scratch_shapes=[
            pltpu.VMEM((tokens, width), bf16),
            pltpu.VMEM((rows_kept, width), bf16),
            pltpu.VMEM((rows_kept, width), bf16),
            pltpu.VMEM(text_keys.shape, bf16),
            pltpu.VMEM(text_keys.shape, bf16),
            pltpu.SMEM((text_rows,), jnp.int32),
            pltpu.VMEM((HEAD_GROUPS, per_source, text_rows, HEAD_DIM), bf16),
            pltpu.VMEM((HEAD_GROUPS, text_rows, HEAD_DIM), bf16),
            pltpu.VMEM((tiles, HEAD_GROUPS * per_source + 1, text_rows, HEAD_DIM), bf16),
            pltpu.VMEM((2, rows_kept, width), bf16),
            pltpu.VMEM((2, rows_kept, width), bf16),
            pltpu.VMEM((tokens, width), bf16),
            pltpu.VMEM((head_count, tokens, HEAD_DIM), f32),
            pltpu.VMEM((head_count, tokens, HEAD_DIM), f32),
            pltpu.VMEM((head_count, tokens, HEAD_DIM), f32),
            dma((6,)),
            dma((head_count,)),
            dma((HEAD_GROUPS, 2)),
            dma((HEAD_GROUPS, 2)),
            dma((2, tiles - 1)),
            dma((2, tiles - 1)),
            dma((2, head_count, 2)),
            dma((2, head_count, 2)),
        ],
        compiler_params=pltpu.CompilerParams(
            collective_id=0, has_side_effects=True, vmem_limit_bytes=56 * 1024 * 1024
        ),
        cost_estimate=pl.CostEstimate(
            flops=4 * tokens * keys_seen * width,
            bytes_accessed=10 * tokens * width,
            transcendentals=tokens * keys_seen * head_count,
        ),
    )(queries, keys, values, text_keys, text_values, text_mask)


def solution(mesh):
    tiles = mesh.shape["tile"] // HEAD_GROUPS

    def shards(*blocks):
        one_row = 1 < tiles <= 4 and blocks[3].shape[0] % 16 == 0
        return (row_shards if one_row else gathered_shards)(*blocks)

    return jax.shard_map(
        shards,
        mesh=mesh,
        in_specs=(
            P(("req", "tile"), None, None),
            P(("req", "tile"), None, None),
            P(("req", "tile"), None, None),
            P(("req", "tile"), None),
            P(("req", "tile"), None),
            P(("req", "tile")),
        ),
        out_specs=P(("req", "tile"), None, None),
        check_vma=False,
    )
```

profile of v0, /device:TPU:0, one launch (start us, length us, event | category | flops | bytes accessed | tf_op | source)
XLA Modules:
  0.0 28.7 jit_solution(6835446438015075161)
XLA Ops:
  0.0 26.9 %shard_map.64 = bf16[1,512,384]{2,1,0:T(8,128)(2,1)} custom-call(bf16[1,512,384]{2,1,0:T(8,128)(2,1)} %q_hbm.1, bf16[1,512,384]{2,1,0:T(8,128)(2,1)} %k_hbm.1, bf16[1,512,384]{2,1,0:T(8,128)(2,1)} %v_hbm.1, bf16[16,1536]{1,0:T(8,128)(2,1)} %tk_hbm.1, bf16[16,1536]{1,0:T(8,128)(2,1)} %tv_hbm.1, s32[16]{0:T(128)} %mask_hbm.1), custom_call_target="tpu_custom_call" | custom-call | flops 1107296256 | bytes 1966080 | tf_op jit(solution)/shard_map/pallas_call | solution.py:414
  26.9 1.8 %copy.8 = bf16[1,512,384]{2,1,0:T(8,128)(2,1)} copy(bf16[1,512,384]{2,1,0:T(8,128)(2,1)} %shard_map.64) | data formatting | bytes 786432
where the time goes:
time: 28.9 us; the launch traced here: 28.7 us
  Pallas kernels  26.9 us (93%)
  local copies, waits for them, and re-layouts  1.78 us (6%)
    pallas_call x1, Pallas kernels, row_shards(): pl.pallas_call(functools.partial(row_kernel, count, rows_kept, head_count...  26.9 us
    unnamed x1, local copies, waits for them, and re-layouts  1.78 us

commit v1 on v0

--- a/solution.py
+++ b/solution.py
@@ -148,10 +148,10 @@
 
 def row_kernel(
     count, rows_kept, head_count, text_rows,
-    q_hbm, k_hbm, v_hbm, tk_hbm, tv_hbm, mask_hbm, out_hbm,
-    q_ref, k_ref, v_ref, tk_ref, tv_ref, mask_ref, packets, flags_in, text, near_k, near_v, out_ref,
-    top_ref, total_ref, summed_ref,
-    in_sem, out_sem, plane_send, plane_recv, chain_send, chain_recv, near_send, near_recv,
+    q_hbm, k_hbm, v_hbm, tk_hbm, tv_hbm, mask_hbm, out_ref,
+    q_ref, k_ref, v_ref, tk_ref, tv_ref, mask_ref, packets, flags_in, text, near_k, near_v,
+    top_ref, total_ref, summed_ref, held_weights, held_top,
+    in_sem, plane_send, plane_recv, chain_send, chain_recv, near_send, near_recv,
 ):
     groups = HEAD_GROUPS
     tiles = count // groups
@@ -265,7 +265,7 @@
             def _():
                 chain_copy(side, hop, owner).wait_recv()
 
-    def fold(head, keys, values, keep, first):
+    def weigh(head, keys, keep, first):
         query = q_ref[:, head * HEAD_DIM : (head + 1) * HEAD_DIM]
         scores = lax.dot_general(query, keys, (((1,), (1,)), ((), ())), preferred_element_type=jnp.float32)
         if keep is not None:
@@ -277,18 +277,26 @@
         ]
         part = functools.reduce(lambda a, b: a + b, pieces)
         weights = jnp.concatenate([piece.astype(jnp.bfloat16) for piece in pieces], axis=1)
-        product = jnp.dot(weights, values, preferred_element_type=jnp.float32)
         if first:
             total_ref[head] = part
-            summed_ref[head] = product
+            summed = None
         else:
             scale_down = jnp.exp2((top_ref[head] - new_top) * EXP2_SCALE)
             total_ref[head] = total_ref[head] * scale_down + part
-            summed_ref[head] = summed_ref[head] * scale_down + product
+            summed = summed_ref[head] * scale_down
         top_ref[head] = new_top
+        return weights, summed
+
+    def fold(head, keys, values, keep, first):
+        weights, summed = weigh(head, keys, keep, first)
+        product = jnp.dot(weights, values, preferred_element_type=jnp.float32)
+        summed_ref[head] = product if summed is None else summed + product
+
+    def head_cols(head):
+        return slice(head * HEAD_DIM, (head + 1) * HEAD_DIM)
 
     def fold_near(head):
-        cols = slice(head * HEAD_DIM, (head + 1) * HEAD_DIM)
+        cols = head_cols(head)
         for side in range(2):
 
             @pl.when(receives[side])
@@ -297,9 +305,40 @@
                     near_copy(side, head, which).wait_recv()
                 fold(head, near_k[side, :, cols], near_v[side, :, cols], None, False)
 
-    def out_copy(head):
-        cols = pl.ds(head * HEAD_DIM, HEAD_DIM)
-        return pltpu.make_async_copy(out_ref.at[:, cols], out_hbm.at[0, :, cols], out_sem.at[head])
+    def weigh_near(head):
+        for side in range(2):
+
+            @pl.when(receives[side])
+            def _():
+                near_copy(side, head, 0).wait_recv()
+                weights, summed = weigh(head, near_k[side, :, head_cols(head)], None, False)
+                summed_ref[head] = summed
+                held_weights[side] = weights
+                held_top[side] = top_ref[head]
+
+    def apply_near(head):
+        for side in range(2):
+
+            @pl.when(receives[side])
+            def _():
+                near_copy(side, head, 1).wait_recv()
+                product = jnp.dot(
+                    held_weights[side], near_v[side, :, head_cols(head)], preferred_element_type=jnp.float32
+                )
+                since = jnp.exp2((held_top[side] - top_ref[head]) * EXP2_SCALE)
+                summed_ref[head] = summed_ref[head] + product * since
+
+    def finish(head):
+        total = jnp.sum(total_ref[head], axis=1, keepdims=True)
+        out_ref[0, :, head_cols(head)] = (summed_ref[head] / total).astype(out_ref.dtype)
+
+    def fold_own(head):
+        fold(head, k_ref[:, head_cols(head)], v_ref[:, head_cols(head)], None, True)
+
+    pl.semaphore_wait(barrier, groups - 1 + has_left.astype(jnp.int32) + has_right.astype(jnp.int32))
+    waiting = [(head, which) for head in range(head_count) for which in range(2)]
+    for item in waiting[:2]:
+        start_near(*item)
 
     loads[0].wait()
     row_of = lax.broadcasted_iota(jnp.int32, (text_rows, HEAD_DIM), 0)
@@ -316,40 +355,34 @@
                 at = (to * head_count + head) * HEAD_DIM
                 packets[to, which * head_count + head] = source[:, at : at + HEAD_DIM]
     text[tile, pl.ds(group * per_source, per_source)] = packets[group]
-
-    pl.semaphore_wait(barrier, groups - 1 + has_left.astype(jnp.int32) + has_right.astype(jnp.int32))
-
     for step in range(1, groups):
         for copy in plane_copies(step):
             copy.start()
-    start_near(0, 0)
-    start_near(0, 1)
+    for load in loads[3:]:
+        load.wait()
+    fold_own(0)
     for step in range(1, groups):
         for copy in plane_copies(step):
             copy.wait_recv()
     text[tile, flag_at] = functools.reduce(lambda a, b: a + b, [flags_in[source] for source in range(groups)])
+
     start_chain(0)
-    start_near(1, 0)
-
-    for load in loads[3:]:
-        load.wait()
-    for head in range(head_count):
-        cols = slice(head * HEAD_DIM, (head + 1) * HEAD_DIM)
-        fold(head, k_ref[:, cols], v_ref[:, cols], None, True)
-
-    rest = [(1, 1)] + [(head, which) for head in range(2, head_count) for which in range(2)]
+    for item in waiting[2:4] if tiles > 2 else waiting[2:]:
+        start_near(*item)
+    for head in range(1, head_count):
+        fold_own(head)
     folded = 0
     for hop in range(1, tiles - 1):
+        if folded < min(2, head_count - 1):
+            fold_near(folded)
+            folded += 1
         wait_chain(hop - 1)
         start_chain(hop)
-        if rest:
-            start_near(*rest.pop(0))
-        if hop == tiles - 2:
-            for item in rest:
-                start_near(*item)
-        if folded < head_count - 1:
-            fold_near(folded)
-            folded += 1
+        for item in waiting[3 + hop : 4 + hop] if hop < tiles - 2 else waiting[3 + hop :]:
+            start_near(*item)
+    for head in range(folded, head_count - 1):
+        fold_near(head)
+    weigh_near(head_count - 1)
     wait_chain(tiles - 2)
 
     wide_row = lax.broadcasted_iota(jnp.int32, (count * text_rows, HEAD_DIM), 0)
@@ -368,14 +401,9 @@
 
     for head in range(head_count):
         fold(head, text_piece(head), text_piece(head_count + head), keep, False)
-
-    for head in range(head_count):
-        if head >= folded:
-            fold_near(head)
-        cols = slice(head * HEAD_DIM, (head + 1) * HEAD_DIM)
-        total = jnp.sum(total_ref[head], axis=1, keepdims=True)
-        out_ref[:, cols] = (summed_ref[head] / total).astype(out_ref.dtype)
-        out_copy(head).start()
+        if head == head_count - 1:
+            apply_near(head)
+        finish(head)
 
     for step in range(1, groups):
         for copy in plane_copies(step):
@@ -394,9 +422,6 @@
             @pl.when(there)
             def _():
                 chain_copy(side, hop, owner).wait_send()
-
-    for head in range(head_count):
-        out_copy(head).wait()
 
 
 def row_shards(queries, keys, values, text_keys, text_values, text_mask):
@@ -413,9 +438,9 @@
     per_source = 2 * head_count
     return pl.pallas_call(
         functools.partial(row_kernel, count, rows_kept, head_count, text_rows),
-        out_shape=jax.ShapeDtypeStruct(queries.shape, bf16),
+        out_shape=pltpu.VMEM(queries.shape, bf16),
         in_specs=[hbm] * 6,
-        out_specs=hbm,
+        out_specs=pl.BlockSpec(memory_space=pltpu.VMEM),
         scratch_shapes=[
             pltpu.VMEM((tokens, width), bf16),
             pltpu.VMEM((rows_kept, width), bf16),
@@ -428,12 +453,12 @@
             pltpu.VMEM((tiles, HEAD_GROUPS * per_source + 1, text_rows, HEAD_DIM), bf16),
             pltpu.VMEM((2, rows_kept, width), bf16),
             pltpu.VMEM((2, rows_kept, width), bf16),
-            pltpu.VMEM((tokens, width), bf16),
             pltpu.VMEM((head_count, tokens, HEAD_DIM), f32),
             pltpu.VMEM((head_count, tokens, HEAD_DIM), f32),
             pltpu.VMEM((head_count, tokens, HEAD_DIM), f32),
+            pltpu.VMEM((2, tokens, rows_kept), bf16),
+            pltpu.VMEM((2, tokens, HEAD_DIM), f32),
             dma((6,)),
-            dma((head_count,)),
             dma((HEAD_GROUPS, 2)),
             dma((HEAD_GROUPS, 2)),
             dma((2, tiles - 1)),

time: 28.9 us -> 26.9 us (0.931)
  local copies, waits for them, and re-layouts: 1.78 us -> 0.75 us
  Pallas kernels: 26.9 us -> 26 us
    unnamed x1, local copies, waits for them, and re-layouts: 1.78 us -> 0.75 us
    pallas_call x1, Pallas kernels: 26.9 us -> 26 us  [row_shards(): pl.pallas_call(functools.partial(row_kernel, count, rows_kept, head_count...]
where the time goes in v1:
time: 26.9 us; the launch traced here: 26.7 us
  Pallas kernels  26 us (97%)
  local copies, waits for them, and re-layouts  0.75 us (3%)
    pallas_call x1, Pallas kernels, row_shards(): pl.pallas_call(functools.partial(row_kernel, count, rows_kept, head_count...  26 us
    unnamed x1, local copies, waits for them, and re-layouts  0.75 us

profile of v1, /device:TPU:0, one launch (start us, length us, event | category | flops | bytes accessed | tf_op | source)
XLA Modules:
  0.0 26.7 jit_solution(5733292579137208588)
XLA Ops:
  0.0 26.0 %shard_map.64 = bf16[1,512,384]{2,1,0:T(8,128)(2,1)S(1)} custom-call(bf16[1,512,384]{2,1,0:T(8,128)(2,1)} %q_hbm.1, bf16[1,512,384]{2,1,0:T(8,128)(2,1)} %k_hbm.1, bf16[1,512,384]{2,1,0:T(8,128)(2,1)} %v_hbm.1, bf16[16,1536]{1,0:T(8,128)(2,1)} %tk_hbm.1, bf16[16,1536]{1,0:T(8,128)(2,1)} %tv_hbm.1, s32[16]{0:T(128)} %mask_hbm.1), custom_call_target="tpu_custom_call" | custom-call | flops 1107296256 | bytes 1966080 | tf_op jit(solution)/shard_map/pallas_call | solution.py:439
  26.0 0.7 %copy.8 = bf16[1,512,384]{2,1,0:T(8,128)(2,1)} copy(bf16[1,512,384]{2,1,0:T(8,128)(2,1)S(1)} %shard_map.64) | data formatting | bytes 786432

commit v2 on v1

--- a/solution.py
+++ b/solution.py
@@ -151,7 +151,7 @@
     q_hbm, k_hbm, v_hbm, tk_hbm, tv_hbm, mask_hbm, out_ref,
     q_ref, k_ref, v_ref, tk_ref, tv_ref, mask_ref, packets, flags_in, text, near_k, near_v,
     top_ref, total_ref, summed_ref, held_weights, held_top,
-    in_sem, plane_send, plane_recv, chain_send, chain_recv, near_send, near_recv,
+    in_sem, plane_send, plane_recv, block_send, block_recv, near_send, near_recv,
 ):
     groups = HEAD_GROUPS
     tiles = count // groups
@@ -161,11 +161,16 @@
     tile = me // groups
     group = lax.rem(me, groups)
     first_here = tile * groups
-    has_left = tile > 0
-    has_right = tile < tiles - 1
-    target = (me + groups, me - groups)
-    sends = (has_right, has_left)
-    receives = (has_left, has_right)
+    far = min(2, tiles - 1)
+
+    def target(side, steps):
+        return me + steps * groups if side == 0 else me - steps * groups
+
+    def sends(side, steps=1):
+        return tile + steps < tiles if side == 0 else tile >= steps
+
+    def receives(side, steps=1):
+        return sends(1 - side, steps)
 
     def partner(step):
         return first_here + lax.rem(group + step, groups)
@@ -173,11 +178,14 @@
     barrier = pltpu.get_barrier_semaphore()
     for step in range(1, groups):
         pl.semaphore_signal(barrier, inc=1, device_id={"tile": partner(step)}, device_id_type=MESH)
+    partners = groups - 1
     for side in range(2):
-
-        @pl.when(sends[side])
-        def _():
-            pl.semaphore_signal(barrier, inc=1, device_id={"tile": target[side]}, device_id_type=MESH)
+        for steps in range(1, far + 1):
+            partners += sends(side, steps).astype(jnp.int32)
+
+            @pl.when(sends(side, steps))
+            def _():
+                pl.semaphore_signal(barrier, inc=1, device_id={"tile": target(side, steps)}, device_id_type=MESH)
 
     loads = [
         pltpu.make_async_copy(mask_hbm, mask_ref, in_sem.at[0]),
@@ -198,14 +206,14 @@
             dst_ref=landing.at[side, :, cols],
             send_sem=near_send.at[side, head, which],
             recv_sem=near_recv.at[side, head, which],
-            device_id={"tile": target[side]},
+            device_id={"tile": target(side, 1)},
             device_id_type=MESH,
         )
 
     def start_near(head, which):
         for side in range(2):
 
-            @pl.when(sends[side])
+            @pl.when(sends(side))
             def _():
                 near_copy(side, head, which).start()
 
@@ -230,40 +238,35 @@
             )
         return made
 
-    def chain_copy(side, hop, owner):
+    def block_copy(side, steps):
+        relayed = steps > far
+        owner = (tile - steps + 1 if side == 0 else tile + steps - 1) if relayed else tile
         return pltpu.make_async_remote_copy(
             src_ref=text.at[owner],
             dst_ref=text.at[owner],
-            send_sem=chain_send.at[side, hop],
-            recv_sem=chain_recv.at[side, hop],
-            device_id={"tile": target[side]},
+            send_sem=block_send.at[side, steps - 1],
+            recv_sem=block_recv.at[side, steps - 1],
+            device_id={"tile": target(side, 1 if relayed else steps)},
             device_id_type=MESH,
         )
 
-    def chain_sent(side, hop):
-        owner = tile - hop if side == 0 else tile + hop
-        there = owner >= 0 if side == 0 else owner < tiles
-        return owner, there & sends[side]
-
-    def chain_got(side, hop):
-        owner = tile - hop - 1 if side == 0 else tile + hop + 1
-        return owner, owner >= 0 if side == 0 else owner < tiles
-
-    def start_chain(hop):
+    def block_sent(side, steps):
+        return sends(side) & receives(side, steps - 1) if steps > far else sends(side, steps)
+
+    def start_block(steps):
         for side in range(2):
-            owner, there = chain_sent(side, hop)
-
-            @pl.when(there)
-            def _():
-                chain_copy(side, hop, owner).start()
-
-    def wait_chain(hop):
+
+            @pl.when(block_sent(side, steps))
+            def _():
+                block_copy(side, steps).start()
+
+    def wait_block(steps):
         for side in range(2):
-            owner, there = chain_got(side, hop)
-
-            @pl.when(there)
-            def _():
-                chain_copy(side, hop, owner).wait_recv()
+
+            @pl.when(receives(side, steps))
+            def _():
+                owner = tile - steps if side == 0 else tile + steps
+                pltpu.make_async_copy(text.at[owner], text.at[owner], block_recv.at[side, steps - 1]).wait()
 
     def weigh(head, keys, keep, first):
         query = q_ref[:, head * HEAD_DIM : (head + 1) * HEAD_DIM]
@@ -299,7 +302,7 @@
         cols = head_cols(head)
         for side in range(2):
 
-            @pl.when(receives[side])
+            @pl.when(receives(side))
             def _():
                 for which in range(2):
                     near_copy(side, head, which).wait_recv()
@@ -308,7 +311,7 @@
     def weigh_near(head):
         for side in range(2):
 
-            @pl.when(receives[side])
+            @pl.when(receives(side))
             def _():
                 near_copy(side, head, 0).wait_recv()
                 weights, summed = weigh(head, near_k[side, :, head_cols(head)], None, False)
@@ -319,7 +322,7 @@
     def apply_near(head):
         for side in range(2):
 
-            @pl.when(receives[side])
+            @pl.when(receives(side))
             def _():
                 near_copy(side, head, 1).wait_recv()
                 product = jnp.dot(
@@ -335,10 +338,9 @@
     def fold_own(head):
         fold(head, k_ref[:, head_cols(head)], v_ref[:, head_cols(head)], None, True)
 
-    pl.semaphore_wait(barrier, groups - 1 + has_left.astype(jnp.int32) + has_right.astype(jnp.int32))
+    pl.semaphore_wait(barrier, partners)
     waiting = [(head, which) for head in range(head_count) for which in range(2)]
-    for item in waiting[:2]:
-        start_near(*item)
+    start_near(*waiting[0])
 
     loads[0].wait()
     row_of = lax.broadcasted_iota(jnp.int32, (text_rows, HEAD_DIM), 0)
@@ -366,24 +368,22 @@
             copy.wait_recv()
     text[tile, flag_at] = functools.reduce(lambda a, b: a + b, [flags_in[source] for source in range(groups)])
 
-    start_chain(0)
-    for item in waiting[2:4] if tiles > 2 else waiting[2:]:
+    for steps in range(1, far + 1):
+        start_block(steps)
+    for item in waiting[1:4]:
         start_near(*item)
     for head in range(1, head_count):
         fold_own(head)
-    folded = 0
-    for hop in range(1, tiles - 1):
-        if folded < min(2, head_count - 1):
-            fold_near(folded)
-            folded += 1
-        wait_chain(hop - 1)
-        start_chain(hop)
-        for item in waiting[3 + hop : 4 + hop] if hop < tiles - 2 else waiting[3 + hop :]:
-            start_near(*item)
-    for head in range(folded, head_count - 1):
+    wait_block(far)
+    for steps in range(far + 1, tiles):
+        start_block(steps)
+    for item in waiting[4:]:
+        start_near(*item)
+    for head in range(head_count - 1):
         fold_near(head)
-    weigh_near(head_count - 1)
-    wait_chain(tiles - 2)
+    for steps in range(1, tiles):
+        if steps != far:
+            wait_block(steps)
 
     wide_row = lax.broadcasted_iota(jnp.int32, (count * text_rows, HEAD_DIM), 0)
     wide_lane = lax.broadcasted_iota(jnp.int32, (count * text_rows, HEAD_DIM), 1)
@@ -402,6 +402,7 @@
     for head in range(head_count):
         fold(head, text_piece(head), text_piece(head_count + head), keep, False)
         if head == head_count - 1:
+            weigh_near(head)
             apply_near(head)
         finish(head)
 
@@ -410,18 +411,17 @@
             copy.wait_send()
     for side in range(2):
 
-        @pl.when(sends[side])
+        @pl.when(sends(side))
         def _():
             for head in range(head_count):
                 for which in range(2):
                     near_copy(side, head, which).wait_send()
 
-        for hop in range(tiles - 1):
-            owner, there = chain_sent(side, hop)
-
-            @pl.when(there)
-            def _():
-                chain_copy(side, hop, owner).wait_send()
+        for steps in range(1, tiles):
+
+            @pl.when(block_sent(side, steps))
+            def _():
+                block_copy(side, steps).wait_send()
 
 
 def row_shards(queries, keys, values, text_keys, text_values, text_mask):

time: 26.9 us -> 29.3 us (1.089)
  Pallas kernels: 26 us -> 28.4 us
    pallas_call x1, Pallas kernels: 26 us -> 28.4 us  [row_shards(): pl.pallas_call(functools.partial(row_kernel, count, rows_kept, head_count...]
where the time goes in v2:
time: 29.3 us; the launch traced here: 29.2 us
  Pallas kernels  28.4 us (97%)
  local copies, waits for them, and re-layouts  0.75 us (3%)
    pallas_call x1, Pallas kernels, row_shards(): pl.pallas_call(functools.partial(row_kernel, count, rows_kept, head_count...  28.4 us
    unnamed x1, local copies, waits for them, and re-layouts  0.75 us

profile of v2, /device:TPU:0, one launch (start us, length us, event | category | flops | bytes accessed | tf_op | source)
XLA Modules:
  0.0 29.2 jit_solution(14513487648595108429)
XLA Ops:
  0.0 28.4 %shard_map.64 = bf16[1,512,384]{2,1,0:T(8,128)(2,1)S(1)} custom-call(bf16[1,512,384]{2,1,0:T(8,128)(2,1)} %q_hbm.1, bf16[1,512,384]{2,1,0:T(8,128)(2,1)} %k_hbm.1, bf16[1,512,384]{2,1,0:T(8,128)(2,1)} %v_hbm.1, bf16[16,1536]{1,0:T(8,128)(2,1)} %tk_hbm.1, bf16[16,1536]{1,0:T(8,128)(2,1)} %tv_hbm.1, s32[16]{0:T(128)} %mask_hbm.1), custom_call_target="tpu_custom_call" | custom-call | flops 1107296256 | bytes 1966080 | tf_op jit(solution)/shard_map/pallas_call | solution.py:439
  28.4 0.7 %copy.8 = bf16[1,512,384]{2,1,0:T(8,128)(2,1)} copy(bf16[1,512,384]{2,1,0:T(8,128)(2,1)S(1)} %shard_map.64) | data formatting | bytes 786432

commit v3 on v1

--- a/solution.py
+++ b/solution.py
@@ -184,18 +184,23 @@
         pltpu.make_async_copy(tk_hbm, tk_ref, in_sem.at[1]),
         pltpu.make_async_copy(tv_hbm, tv_ref, in_sem.at[2]),
         pltpu.make_async_copy(q_hbm.at[0], q_ref, in_sem.at[3]),
-        pltpu.make_async_copy(k_hbm.at[0, pl.ds(0, rows_kept), :], k_ref, in_sem.at[4]),
-        pltpu.make_async_copy(v_hbm.at[0, pl.ds(0, rows_kept), :], v_ref, in_sem.at[5]),
     ]
+    for which, (source, landing) in enumerate(((k_hbm, k_ref), (v_hbm, v_ref))):
+        for head in range(head_count):
+            cols = pl.ds(head * HEAD_DIM, HEAD_DIM)
+            loads.append(
+                pltpu.make_async_copy(
+                    source.at[0, pl.ds(0, rows_kept), cols], landing.at[head], in_sem.at[4 + which * head_count + head]
+                )
+            )
     for load in loads:
         load.start()
 
     def near_copy(side, head, which):
-        cols = pl.ds(head * HEAD_DIM, HEAD_DIM)
-        source, landing = ((k_hbm, near_k), (v_hbm, near_v))[which]
+        source, landing = ((k_ref, near_k), (v_ref, near_v))[which]
         return pltpu.make_async_remote_copy(
-            src_ref=source.at[0, pl.ds(0, rows_kept), cols],
-            dst_ref=landing.at[side, :, cols],
+            src_ref=source.at[head],
+            dst_ref=landing.at[side, head],
             send_sem=near_send.at[side, head, which],
             recv_sem=near_recv.at[side, head, which],
             device_id={"tile": target[side]},
@@ -296,14 +301,13 @@
         return slice(head * HEAD_DIM, (head + 1) * HEAD_DIM)
 
     def fold_near(head):
-        cols = head_cols(head)
         for side in range(2):
 
             @pl.when(receives[side])
             def _():
                 for which in range(2):
                     near_copy(side, head, which).wait_recv()
-                fold(head, near_k[side, :, cols], near_v[side, :, cols], None, False)
+                fold(head, near_k[side, head], near_v[side, head], None, False)
 
     def weigh_near(head):
         for side in range(2):
@@ -311,7 +315,7 @@
             @pl.when(receives[side])
             def _():
                 near_copy(side, head, 0).wait_recv()
-                weights, summed = weigh(head, near_k[side, :, head_cols(head)], None, False)
+                weights, summed = weigh(head, near_k[side, head], None, False)
                 summed_ref[head] = summed
                 held_weights[side] = weights
                 held_top[side] = top_ref[head]
@@ -323,7 +327,7 @@
             def _():
                 near_copy(side, head, 1).wait_recv()
                 product = jnp.dot(
-                    held_weights[side], near_v[side, :, head_cols(head)], preferred_element_type=jnp.float32
+                    held_weights[side], near_v[side, head], preferred_element_type=jnp.float32
                 )
                 since = jnp.exp2((held_top[side] - top_ref[head]) * EXP2_SCALE)
                 summed_ref[head] = summed_ref[head] + product * since
@@ -333,12 +337,13 @@
         out_ref[0, :, head_cols(head)] = (summed_ref[head] / total).astype(out_ref.dtype)
 
     def fold_own(head):
-        fold(head, k_ref[:, head_cols(head)], v_ref[:, head_cols(head)], None, True)
+        fold(head, k_ref[head], v_ref[head], None, True)
 
     pl.semaphore_wait(barrier, groups - 1 + has_left.astype(jnp.int32) + has_right.astype(jnp.int32))
     waiting = [(head, which) for head in range(head_count) for which in range(2)]
-    for item in waiting[:2]:
-        start_near(*item)
+    for load in loads[3:]:
+        load.wait()
+    start_near(*waiting[0])
 
     loads[0].wait()
     row_of = lax.broadcasted_iota(jnp.int32, (text_rows, HEAD_DIM), 0)
@@ -358,8 +363,6 @@
     for step in range(1, groups):
         for copy in plane_copies(step):
             copy.start()
-    for load in loads[3:]:
-        load.wait()
     fold_own(0)
     for step in range(1, groups):
         for copy in plane_copies(step):
@@ -367,22 +370,20 @@
     text[tile, flag_at] = functools.reduce(lambda a, b: a + b, [flags_in[source] for source in range(groups)])
 
     start_chain(0)
-    for item in waiting[2:4] if tiles > 2 else waiting[2:]:
+    for item in waiting[1:3]:
         start_near(*item)
     for head in range(1, head_count):
         fold_own(head)
-    folded = 0
     for hop in range(1, tiles - 1):
-        if folded < min(2, head_count - 1):
-            fold_near(folded)
-            folded += 1
         wait_chain(hop - 1)
         start_chain(hop)
-        for item in waiting[3 + hop : 4 + hop] if hop < tiles - 2 else waiting[3 + hop :]:
-            start_near(*item)
-    for head in range(folded, head_count - 1):
+        start_near(*waiting[2 + hop])
+        if hop == 1:
+            fold_near(0)
+    for item in waiting[1 + tiles :]:
+        start_near(*item)
+    for head in range(1 if tiles > 2 else 0, head_count - 1):
         fold_near(head)
-    weigh_near(head_count - 1)
     wait_chain(tiles - 2)
 
     wide_row = lax.broadcasted_iota(jnp.int32, (count * text_rows, HEAD_DIM), 0)
@@ -402,6 +403,7 @@
     for head in range(head_count):
         fold(head, text_piece(head), text_piece(head_count + head), keep, False)
         if head == head_count - 1:
+            weigh_near(head)
             apply_near(head)
         finish(head)
 
@@ -443,22 +445,22 @@
         out_specs=pl.BlockSpec(memory_space=pltpu.VMEM),
         scratch_shapes=[
             pltpu.VMEM((tokens, width), bf16),
-            pltpu.VMEM((rows_kept, width), bf16),
-            pltpu.VMEM((rows_kept, width), bf16),
+            pltpu.VMEM((head_count, rows_kept, HEAD_DIM), bf16),
+            pltpu.VMEM((head_count, rows_kept, HEAD_DIM), bf16),
             pltpu.VMEM(text_keys.shape, bf16),
             pltpu.VMEM(text_keys.shape, bf16),
             pltpu.SMEM((text_rows,), jnp.int32),
             pltpu.VMEM((HEAD_GROUPS, per_source, text_rows, HEAD_DIM), bf16),
             pltpu.VMEM((HEAD_GROUPS, text_rows, HEAD_DIM), bf16),
             pltpu.VMEM((tiles, HEAD_GROUPS * per_source + 1, text_rows, HEAD_DIM), bf16),
-            pltpu.VMEM((2, rows_kept, width), bf16),
-            pltpu.VMEM((2, rows_kept, width), bf16),
+            pltpu.VMEM((2, head_count, rows_kept, HEAD_DIM), bf16),
+            pltpu.VMEM((2, head_count, rows_kept, HEAD_DIM), bf16),
             pltpu.VMEM((head_count, tokens, HEAD_DIM), f32),
             pltpu.VMEM((head_count, tokens, HEAD_DIM), f32),
             pltpu.VMEM((head_count, tokens, HEAD_DIM), f32),
             pltpu.VMEM((2, tokens, rows_kept), bf16),
             pltpu.VMEM((2, tokens, HEAD_DIM), f32),
-            dma((6,)),
+            dma((4 + 2 * head_count,)),
             dma((HEAD_GROUPS, 2)),
             dma((HEAD_GROUPS, 2)),
             dma((2, tiles - 1)),

time: 26.9 us -> 28.5 us (1.059)
  Pallas kernels: 26 us -> 27.6 us
    pallas_call x1, Pallas kernels: 26 us -> 27.6 us  [row_shards(): pl.pallas_call(functools.partial(row_kernel, count, rows_kept, head_count...]
where the time goes in v3:
time: 28.5 us; the launch traced here: 28.3 us
  Pallas kernels  27.6 us (97%)
  local copies, waits for them, and re-layouts  0.75 us (3%)
    pallas_call x1, Pallas kernels, row_shards(): pl.pallas_call(functools.partial(row_kernel, count, rows_kept, head_count...  27.6 us
    unnamed x1, local copies, waits for them, and re-layouts  0.75 us

profile of v3, /device:TPU:0, one launch (start us, length us, event | category | flops | bytes accessed | tf_op | source)
XLA Modules:
  0.0 28.3 jit_solution(16636887394635970726)
XLA Ops:
  0.0 27.6 %shard_map.64 = bf16[1,512,384]{2,1,0:T(8,128)(2,1)S(1)} custom-call(bf16[1,512,384]{2,1,0:T(8,128)(2,1)} %q_hbm.1, bf16[1,512,384]{2,1,0:T(8,128)(2,1)} %k_hbm.1, bf16[1,512,384]{2,1,0:T(8,128)(2,1)} %v_hbm.1, bf16[16,1536]{1,0:T(8,128)(2,1)} %tk_hbm.1, bf16[16,1536]{1,0:T(8,128)(2,1)} %tv_hbm.1, s32[16]{0:T(128)} %mask_hbm.1), custom_call_target="tpu_custom_call" | custom-call | flops 1107296256 | bytes 1966080 | tf_op jit(solution)/shard_map/pallas_call | solution.py:441
  27.6 0.7 %copy.8 = bf16[1,512,384]{2,1,0:T(8,128)(2,1)} copy(bf16[1,512,384]{2,1,0:T(8,128)(2,1)S(1)} %shard_map.64) | data formatting | bytes 786432
